TPU v7x, 32 devices: a whole 2x2x4 slice. The times are simulated.
32 devices in a mesh: tm: 8 (over z, y), space: 4 (over x, core).
Axes of the slice: x: 2, y: 2, z: 4, core: 2. Of those that a mesh axis runs over, the one named last changes fastest.
Arguments:
- initial_field: float32 [32, 8, 512], P('space'), may hold values from -1.2 to 1.2
- mobility: float32 [32, 8, 512], P('space'), may hold values from 0.25 to 1
Outputs:
- ends: float32 [8, 32, 8, 512], P('tm', 'space')
All inputs are finite; a program needn't handle non-finite values.
Results may differ from a plain program's by a relative error of at most 0.0001.
Values sent between devices are 32-bit elements; how exact they have to be, the bound alone decides.
A program may use at most 64 MiB of HBM per device.

v0:
```python
import jax
import jax.numpy as jnp
from jax import lax
from jax.sharding import PartitionSpec as P

ITERS = 2


gradient_coef = 1.0
slice_step = 0.016
half_step = 0.008
coarse_scale = 0.25


def with_halo(array, sides, width):
    for axis, dim in sides:
        size, length = (lax.axis_size(axis), array.shape[dim])
        up = [(i, (i + 1) % size) for i in range(size)]
        down = [(j, i) for i, j in up]
        last = lax.slice_in_dim(array, length - width, length, axis=dim)
        leading = lax.slice_in_dim(array, 0, width, axis=dim)
        before = lax.ppermute(last, axis, up)
        after = lax.ppermute(leading, axis, down)
        array = jnp.concatenate([before, array, after], axis=dim)
    return array


def passed_along(array, axis, by):
    length = lax.axis_size(axis)
    pairs = [(i, i + by) for i in range(length) if 0 <= i + by < length]
    return lax.ppermute(array, axis, pairs)


def chemical_flow(values, coefficient, inv_spacing):
    interior = values[..., 1:-1, :, :]
    laplace = (
        values[..., 2:, :, :]
        + values[..., :-2, :, :]
        + jnp.roll(interior, 1, -2)
        + jnp.roll(interior, -1, -2)
        + jnp.roll(interior, 1, -1)
        + jnp.roll(interior, -1, -1)
        - 6.0 * interior
    ) * inv_spacing
    potential = interior * interior * interior - interior - gradient_coef * laplace
    mobile = coefficient[..., 1:-1, :, :] * jnp.maximum(1.0 - interior * interior, 0.0)
    face_z = (
        0.5
        * (mobile[..., 1:, :, :] + mobile[..., :-1, :, :])
        * (potential[..., 1:, :, :] - potential[..., :-1, :, :])
    )
    centre_pot = potential[..., 1:-1, :, :]
    centre_mob = mobile[..., 1:-1, :, :]
    face_y = (
        0.5
        * (jnp.roll(centre_mob, -1, -2) + centre_mob)
        * (jnp.roll(centre_pot, -1, -2) - centre_pot)
    )
    face_x = (
        0.5
        * (jnp.roll(centre_mob, -1, -1) + centre_mob)
        * (jnp.roll(centre_pot, -1, -1) - centre_pot)
    )
    summed = (
        face_z[..., 1:, :, :]
        - face_z[..., :-1, :, :]
        + (face_y - jnp.roll(face_y, 1, -2))
        + (face_x - jnp.roll(face_x, 1, -1))
    )
    return summed * inv_spacing


def planar_flow(values, coefficient, inv_spacing):
    laplace = (
        jnp.roll(values, 1, -2)
        + jnp.roll(values, -1, -2)
        + jnp.roll(values, 1, -1)
        + jnp.roll(values, -1, -1)
        - 4.0 * values
    ) * inv_spacing
    potential = values * values * values - values - gradient_coef * laplace
    mobile = coefficient * jnp.maximum(1.0 - values * values, 0.0)
    face_y = 0.5 * (jnp.roll(mobile, -1, -2) + mobile) * (jnp.roll(potential, -1, -2) - potential)
    face_x = 0.5 * (jnp.roll(mobile, -1, -1) + mobile) * (jnp.roll(potential, -1, -1) - potential)
    summed = face_y - jnp.roll(face_y, 1, -2) + (face_x - jnp.roll(face_x, 1, -1))
    return summed * inv_spacing


def trim_planes(values, margin):
    return values[..., margin : values.shape[-3] - margin, :, :]


def restrict(values):
    leading = values.shape[:-3]
    plane_count, row_count, col_count = values.shape[-3:]
    blocks = values.reshape(leading + (plane_count // 2, 2, row_count // 2, 2, col_count // 2, 2))
    return jnp.sum(blocks, axis=(-5, -3, -1)) * 0.125


def prolong(coarse):
    leading = coarse.shape[:-3]
    plane_count, row_count, col_count = coarse.shape[-3:]
    spread = jnp.broadcast_to(
        coarse[..., :, None, :, None, :, None],
        leading + (plane_count, 2, row_count, 2, col_count, 2),
    )
    return spread.reshape(leading + (2 * plane_count, 2 * row_count, 2 * col_count))


def widen_slab(values, margin):
    return with_halo(values, (("space", 1),), margin)


def on_device(initial_field, mobility):
    planes = initial_field.shape[0]
    margin_cells = 2
    time_rank = lax.axis_index("tm")
    slice_count = lax.axis_size("tm")
    opened = widen_slab(jnp.stack([initial_field, mobility]), margin_cells)
    initial_wide = opened[0]
    mobility_wide = opened[1]

    def centred(values):
        return trim_planes(values, (values.shape[-3] - planes) // 2)

    def evaluate(values):
        widened = widen_slab(values[None], 2)[0]
        return chemical_flow(widened, trim_planes(mobility_wide, margin_cells - 2), 1.0)

    coarse_mobility = restrict(mobility)
    first_coarse = restrict(initial_field)

    def coarse_force(values):
        return planar_flow(values, coarse_mobility, coarse_scale)

    def coarse_sweep(values, forcing_here):
        return values + slice_step * coarse_force(values) + forcing_here

    first_force = chemical_flow(initial_wide, mobility_wide, 1.0)
    force_set = (first_force, first_force, first_force)
    node_zero = trim_planes(initial_wide, 2)
    next_zero = initial_field
    node_one = initial_field
    node_two = initial_field
    for sweep_index in range(ITERS):
        if sweep_index > 0:
            stacked = widen_slab(jnp.stack([next_zero, node_one, node_two]), margin_cells)
            all_forces = chemical_flow(stacked, mobility_wide, 1.0)
            force_set = (all_forces[0], all_forces[1], all_forces[2])
            node_zero = trim_planes(stacked[0], 2)
        f_zero, f_one, f_two = force_set
        middle = node_zero + slice_step * (
            5.0 / 24.0 * f_zero + 1.0 / 3.0 * f_one - 1.0 / 24.0 * f_two
        )
        middle_force = evaluate(middle)
        shrink_by = (middle.shape[-3] - middle_force.shape[-3]) // 2
        ending = (
            trim_planes(middle, shrink_by)
            + half_step * (middle_force - trim_planes(f_one, shrink_by))
            + slice_step
            * (
                -(1.0 / 24.0) * trim_planes(f_zero, shrink_by)
                + 1.0 / 3.0 * trim_planes(f_one, shrink_by)
                + 5.0 / 24.0 * trim_planes(f_two, shrink_by)
            )
        )
        ending_force = evaluate(ending)
        middle = centred(middle)
        middle_force = centred(middle_force)
        ending = centred(ending)
        f_zero = centred(f_zero)
        node_zero = centred(node_zero)
        coarse_zero = restrict(node_zero)
        coarse_one = restrict(ending)
        integral = restrict(slice_step / 6.0 * (f_zero + 4.0 * middle_force + ending_force))
        forcing = integral - slice_step * coarse_force(coarse_zero)
        all_forcing = lax.all_gather(forcing[None], "tm", axis=0, tiled=True)
        paired = all_forcing.reshape((slice_count // 2, 2) + forcing.shape)

        def replay_turn(step_index, state_now):
            current, owned_zero, owned_one = state_now
            for within in range(2):
                rank_here = 2 * step_index + within
                advanced = coarse_sweep(current, paired[step_index, within])
                owned_zero = jnp.where(rank_here == time_rank, current, owned_zero)
                owned_one = jnp.where(rank_here == time_rank, advanced, owned_one)
                current = advanced
            return (current, owned_zero, owned_one)

        empty_state = jnp.zeros_like(forcing)
        finished, own_zero, own_one = lax.fori_loop(
            0, slice_count // 2, replay_turn, (first_coarse, empty_state, empty_state)
        )
        node_one = middle + prolong(0.5 * (own_zero - coarse_zero + (own_one - coarse_one)))
        node_two = ending + prolong(own_one - coarse_one)
        if sweep_index + 1 < ITERS:
            incoming = passed_along(node_two, "tm", 1)
            next_zero = jnp.where(time_rank == 0, initial_field, incoming)
    return node_two[None]


def solution(mesh):
    in_specs = (P("space", None, None), P("space", None, None))
    out_specs = P("tm", "space", None, None)
    return jax.shard_map(
        on_device, mesh=mesh, in_specs=in_specs, out_specs=out_specs, check_vma=False
    )
```

profile of v0, /device:TPU:0, one launch (start us, length us, event | category | flops | bytes accessed | tf_op | source)
XLA Modules:
  0.0 238.4 jit_solution(13379879171976971093)
XLA Ops:
  0.0 0.8 pad_maximum_fusion.28
  0.8 0.5 collective-permute-start
  1.3 2.0 collective-permute-start.1
  3.3 10.5 %reshape.803 = f32[4,2,4,2,256,2]{5,4,3,2,1,0:T(8,128)} reshape(f32[8,8,512]{2,1,0:T(8,128)} %param.6) | data formatting | bytes 262144 | tf_op jit(solution)/shard_map/reshape | solution.py:96
  13.9 4.0 %reduce_sum.67 = f32[4,4,256]{2,1,0:T(4,128)S(1)} reduce(f32[4,2,4,2,256,2]{5,4,3,2,1,0:T(8,128)} %reshape.803, f32[]{:T(128)} %constant.251.clone.1), dimensions={1,3,5}, to_apply=%region_0.0 | reduce | flops 28672 | bytes 147460 | tf_op jit(solution)/shard_map/reduce_sum | solution.py:97
  18.1 9.8 %reshape.804 = f32[4,2,4,2,256,2]{5,4,3,2,1,0:T(8,128)} reshape(f32[8,8,512]{2,1,0:T(8,128)S(1)} %copy-done.4) | data formatting | bytes 262144 | tf_op jit(solution)/shard_map/reshape | solution.py:96
  27.9 4.0 %reduce_sum.68 = f32[4,4,256]{2,1,0:T(4,128)S(1)} reduce(f32[4,2,4,2,256,2]{5,4,3,2,1,0:T(8,128)} %reshape.804, f32[]{:T(128)} %constant.251.clone.1), dimensions={1,3,5}, to_apply=%region_2.3 | reduce | flops 28672 | bytes 147460 | tf_op jit(solution)/shard_map/reduce_sum | solution.py:97
  33.5 0.7 collective-permute-start.2
  34.2 1.1 collective-permute-start.3
  35.3 1.6 collective-permute-done.2
  37.2 0.2 fusion.92
  38.1 2.3 collective-permute-start.4
  40.5 9.8 %reshape.807 = f32[4,2,4,2,256,2]{5,4,3,2,1,0:T(8,128)} reshape(f32[8,8,512]{2,1,0:T(8,128)S(1)} %get-tuple-element.460) | data formatting | bytes 262144 | tf_op jit(solution)/shard_map/reshape | solution.py:96
  50.3 4.0 %reduce_sum.70 = f32[4,4,256]{2,1,0:T(4,128)S(1)} reduce(f32[4,2,4,2,256,2]{5,4,3,2,1,0:T(8,128)} %reshape.807, f32[]{:T(128)} %constant.251.clone.1), dimensions={1,3,5}, to_apply=%region_5.6 | reduce | flops 28672 | bytes 147460 | tf_op jit(solution)/shard_map/reduce_sum | solution.py:97
  54.6 0.2 fusion.86
  55.5 9.8 %reshape.805 = f32[4,2,4,2,256,2]{5,4,3,2,1,0:T(8,128)} reshape(f32[8,8,512]{2,1,0:T(8,128)S(1)} %fusion.151) | data formatting | bytes 262144 | tf_op jit(solution)/shard_map/reshape | solution.py:96
  65.3 4.0 %reduce_sum.69 = f32[4,4,256]{2,1,0:T(4,128)S(1)} reduce(f32[4,2,4,2,256,2]{5,4,3,2,1,0:T(8,128)} %reshape.805, f32[]{:T(128)} %constant.251.clone.1), dimensions={1,3,5}, to_apply=%region_1.0 | reduce | flops 28672 | bytes 147460 | tf_op jit(solution)/shard_map/reduce_sum | solution.py:97
  69.4 31.2 %all_gather.6 = f32[8,4,4,256]{3,2,1,0:T(4,128)S(1)} all-gather(f32[1,4,4,256]{3,2,1,0:T(4,128)S(1)} %fusion.201), channel_id=1, replica_groups=mesh['tm'=8,'space'=4] {'tm'}, dimensions={0}, use_global_device_ids=true | all-gather | bytes 147456 | tf_op jit(solution)/shard_map/all_gather | solution.py:177
  100.7 6.0 %while.40 = (s32[]{:T(128)}, f32[4,4,256]{2,1,0:T(4,128)S(1)}, f32[4,4,256]{2,1,0:T(4,128)S(1)}, f32[4,4,256]{2,1,0:T(4,128)S(1)}, f32[4,4,256]{2,1,0:T(4,128)S(...) while((s32[]{:T(128)}, f32[4,4,256]{2,1,0:T(4,128)S(1)}, ...), condition=%wide.region_4.5_spmd.clone, body=%wide.region_3.4_spmd.clone.sunk | while | flops 327687 | bytes 1360294 | solution.py:191
  106.7 3.9 %broadcast_in_dim.16 = f32[4,2,4,2,256,2]{5,4,3,2,1,0:T(8,128)} broadcast(f32[4,4,256]{2,1,0:T(4,128)S(1)} %get-tuple-element.459), dimensions={0,2,4} | broadcast | bytes 147456 | tf_op jit(solution)/shard_map/broadcast_in_dim | solution.py:103
  110.6 6.9 %reshape.808 = f32[8,8,512]{2,1,0:T(8,128)S(1)} reshape(f32[4,2,4,2,256,2]{5,4,3,2,1,0:T(8,128)} %broadcast_in_dim.16) | data formatting | bytes 262144 | tf_op jit(solution)/shard_map/reshape | solution.py:107
  117.6 3.4 %collective-permute-start.6 = (f32[8,8,512]{2,1,0:T(8,128)S(1)}, f32[8,8,512]{2,1,0:T(8,128)S(1)}, u32[]{:S(2)}, u32[]{:S(2)}) collective-permute-start(f32[8,8,512]{2,1,0:T(8,128)S(1)} %add.889), channel_id=1, source_target_pairs={{0,4},{4,8},{8,12},{12,16},{16,20},{20,24},{24,28},{1,5},{5,9},{9,... | collective-permute-start | bytes 393224 | tf_op jit(solution)/shard_map/ppermute | solution.py:31
  121.0 3.9 %broadcast_in_dim.17 = f32[4,2,4,2,256,2]{5,4,3,2,1,0:T(8,128)} broadcast(f32[4,4,256]{2,1,0:T(4,128)S(1)} %get-tuple-element.458), dimensions={0,2,4} | broadcast | bytes 147456 | tf_op jit(solution)/shard_map/broadcast_in_dim | solution.py:103
  124.9 6.9 %reshape.809 = f32[8,8,512]{2,1,0:T(8,128)S(1)} reshape(f32[4,2,4,2,256,2]{5,4,3,2,1,0:T(8,128)} %broadcast_in_dim.17) | data formatting | bytes 262144 | tf_op jit(solution)/shard_map/reshape | solution.py:107
  132.0 9.8 %reshape.811 = f32[4,2,4,2,256,2]{5,4,3,2,1,0:T(8,128)} reshape(f32[8,8,512]{2,1,0:T(8,128)S(1)} %get-tuple-element.588) | data formatting | bytes 262144 | tf_op jit(solution)/shard_map/reshape | solution.py:96
  141.7 4.0 %reduce_sum.72 = f32[4,4,256]{2,1,0:T(4,128)S(1)} reduce(f32[4,2,4,2,256,2]{5,4,3,2,1,0:T(8,128)} %reshape.811, f32[]{:T(128)} %constant.251.clone.1), dimensions={1,3,5}, to_apply=%region_7.8 | reduce | flops 28672 | bytes 147460 | tf_op jit(solution)/shard_map/reduce_sum | solution.py:97
  146.4 1.7 collective-permute-start.8
  148.2 2.2 collective-permute-done.7
  150.5 0.2 fusion.263
  151.0 0.4 fusion.65
  151.4 0.2 slice.2255
  152.1 0.4 fusion.80
  152.6 0.2 fusion.76
  152.9 2.0 collective-permute-start.10
  154.9 1.6 collective-permute-done.10
  156.5 1.9 collective-permute-done.9
  158.7 0.2 fusion.94
  159.7 1.7 collective-permute-start.12
  161.5 9.8 %reshape.813 = f32[4,2,4,2,256,2]{5,4,3,2,1,0:T(8,128)} reshape(f32[8,8,512]{2,1,0:T(8,128)S(1)} %get-tuple-element.456) | data formatting | bytes 262144 | tf_op jit(solution)/shard_map/reshape | solution.py:96
  171.2 4.0 %reduce_sum.73 = f32[4,4,256]{2,1,0:T(4,128)S(1)} reduce(f32[4,2,4,2,256,2]{5,4,3,2,1,0:T(8,128)} %reshape.813, f32[]{:T(128)} %constant.251.clone.1), dimensions={1,3,5}, to_apply=%region_10.11 | reduce | flops 28672 | bytes 147460 | tf_op jit(solution)/shard_map/reduce_sum | solution.py:97
  175.6 0.2 fusion.90
  176.4 9.8 %reshape.810 = f32[4,2,4,2,256,2]{5,4,3,2,1,0:T(8,128)} reshape(f32[8,8,512]{2,1,0:T(8,128)S(1)} %fusion.145) | data formatting | bytes 262144 | tf_op jit(solution)/shard_map/reshape | solution.py:96
  186.2 4.0 %reduce_sum.71 = f32[4,4,256]{2,1,0:T(4,128)S(1)} reduce(f32[4,2,4,2,256,2]{5,4,3,2,1,0:T(8,128)} %reshape.810, f32[]{:T(128)} %constant.251.clone.1), dimensions={1,3,5}, to_apply=%region_6.7 | reduce | flops 28672 | bytes 147460 | tf_op jit(solution)/shard_map/reduce_sum | solution.py:97
  190.4 30.5 %all_gather.7 = f32[8,4,4,256]{3,2,1,0:T(4,128)S(1)} all-gather(f32[1,4,4,256]{3,2,1,0:T(4,128)S(1)} %fusion.222), channel_id=1, replica_groups=mesh['tm'=8,'space'=4] {'tm'}, dimensions={0}, use_global_device_ids=true | all-gather | bytes 147456 | tf_op jit(solution)/shard_map/all_gather | solution.py:177
  220.9 6.0 %while.41 = (s32[]{:T(128)}, f32[4,4,256]{2,1,0:T(4,128)S(1)}, f32[4,4,256]{2,1,0:T(4,128)S(1)}, f32[4,4,256]{2,1,0:T(4,128)S(1)}, f32[4,2,4,4,256]{4,3,2,1,0:T(...) while((s32[]{:T(128)}, f32[4,4,256]{2,1,0:T(4,128)S(1)}, ...), condition=%wide.region_9.10_spmd.clone, body=%wide.region_8.9_spmd.clone.sunk | while | flops 319495 | bytes 1327515 | solution.py:191
  226.9 3.9 %broadcast_in_dim.19 = f32[4,2,4,2,256,2]{5,4,3,2,1,0:T(8,128)} broadcast(f32[4,4,256]{2,1,0:T(4,128)S(1)} %multiply_subtract_fusion.28), dimensions={0,2,4} | broadcast | bytes 147456 | tf_op jit(solution)/shard_map/broadcast_in_dim | solution.py:103
  230.8 6.9 %reshape.814 = f32[8,8,512]{2,1,0:T(8,128)S(1)} reshape(f32[4,2,4,2,256,2]{5,4,3,2,1,0:T(8,128)} %broadcast_in_dim.19) | data formatting | bytes 262144 | tf_op jit(solution)/shard_map/reshape | solution.py:107
  237.7 0.7 add_bitcast_fusion
  (449 shorter events, 18.3 us)
Async XLA Ops:
  0.8 31.5 %collective-permute-start = (f32[2,2,8,512]{3,2,1,0:T(8,128)S(1)}, f32[2,2,8,512]{3,2,1,0:T(8,128)S(1)}, u32[]{:S(2)}, u32[]{:S(2)}) collective-permute-start(f32[2,2,8,512]{3,2,1,0:T(8,128)S(1)} %get-tuple-element.533), channel_id=1, source_target_pairs={{0,1},{1,2},{2,3},{3,0},{4,5},{5,6},{6,7},{7,4},{8,9},{9,10},{10,1... | collective-permute-start | bytes 196616 | tf_op jit(solution)/shard_map/ppermute | solution.py:22
  1.3 16.8 %copy-start.4 = (f32[8,8,512]{2,1,0:T(8,128)S(1)}, f32[8,8,512]{2,1,0:T(8,128)}, u32[]{:S(2)}) copy-start(f32[8,8,512]{2,1,0:T(8,128)} %param.7) | copy-start | bytes 393220
  1.3 31.0 %collective-permute-start.1 = (f32[2,2,8,512]{3,2,1,0:T(8,128)S(1)}, f32[2,2,8,512]{3,2,1,0:T(8,128)S(1)}, u32[]{:S(2)}, u32[]{:S(2)}) collective-permute-start(f32[2,2,8,512]{3,2,1,0:T(8,128)S(1)} %get-tuple-element.534), channel_id=1, source_target_pairs={{1,0},{2,1},{3,2},{0,3},{5,4},{6,5},{7,6},{4,7},{9,8},{10,9},{11,1... | collective-permute-start | bytes 196616 | tf_op jit(solution)/shard_map/ppermute | solution.py:23
  17.9 22.6 %copy-start = (f32[4,4,256]{2,1,0:T(4,128)}, f32[4,4,256]{2,1,0:T(4,128)S(1)}, u32[]{:S(2)}) copy-start(f32[4,4,256]{2,1,0:T(4,128)S(1)} %broadcast_multiply_fusion.2) | copy-start | bytes 49156
  18.1 14.2 %copy-start.3 = (f32[8,8,512]{2,1,0:T(8,128)S(1)}, f32[8,8,512]{2,1,0:T(8,128)}, u32[]{:S(2)}) copy-start(f32[8,8,512]{2,1,0:T(8,128)} %param.6) | copy-start | bytes 393220
  33.5 3.4 %collective-permute-start.2 = (f32[1,2,8,512]{3,2,1,0:T(8,128)S(1)}, f32[1,2,8,512]{3,2,1,0:T(8,128)S(1)}, u32[]{:S(2)}, u32[]{:S(2)}) collective-permute-start(f32[1,2,8,512]{3,2,1,0:T(8,128)S(1)} %get-tuple-element.591), channel_id=1, source_target_pairs={{0,1},{1,2},{2,3},{3,0},{4,5},{5,6},{6,7},{7,4},{8,9},{9,10},{10,1... | collective-permute-start | bytes 98312 | tf_op jit(solution)/shard_map/ppermute | solution.py:22
  34.2 2.8 %collective-permute-start.3 = (f32[1,2,8,512]{3,2,1,0:T(8,128)S(1)}, f32[1,2,8,512]{3,2,1,0:T(8,128)S(1)}, u32[]{:S(2)}, u32[]{:S(2)}) collective-permute-start(f32[1,2,8,512]{3,2,1,0:T(8,128)S(1)} %get-tuple-element.592), channel_id=1, source_target_pairs={{1,0},{2,1},{3,2},{0,3},{5,4},{6,5},{7,6},{4,7},{9,8},{10,9},{11,1... | collective-permute-start | bytes 98312 | tf_op jit(solution)/shard_map/ppermute | solution.py:23
  38.1 16.2 %collective-permute-start.4 = (f32[1,2,8,512]{3,2,1,0:T(8,128)S(1)}, f32[1,2,8,512]{3,2,1,0:T(8,128)S(1)}, u32[]{:S(2)}, u32[]{:S(2)}) collective-permute-start(f32[1,2,8,512]{3,2,1,0:T(8,128)S(1)} %get-tuple-element.589), channel_id=1, source_target_pairs={{0,1},{1,2},{2,3},{3,0},{4,5},{5,6},{6,7},{7,4},{8,9},{9,10},{10,1... | collective-permute-start | bytes 98312 | tf_op jit(solution)/shard_map/ppermute | solution.py:22
  40.4 13.9 %collective-permute-start.5 = (f32[1,2,8,512]{3,2,1,0:T(8,128)S(1)}, f32[1,2,8,512]{3,2,1,0:T(8,128)S(1)}, u32[]{:S(2)}, u32[]{:S(2)}) collective-permute-start(f32[1,2,8,512]{3,2,1,0:T(8,128)S(1)} %get-tuple-element.590), channel_id=1, source_target_pairs={{1,0},{2,1},{3,2},{0,3},{5,4},{6,5},{7,6},{4,7},{9,8},{10,9},{11,1... | collective-permute-start | bytes 98312 | tf_op jit(solution)/shard_map/ppermute | solution.py:23
  55.5 45.2 %copy-start.2 = (f32[4,4,256]{2,1,0:T(4,128)S(1)}, f32[4,4,256]{2,1,0:T(4,128)}, u32[]{:S(2)}) copy-start(f32[4,4,256]{2,1,0:T(4,128)} %copy-done) | copy-start | bytes 49156
  117.6 14.3 %collective-permute-start.6 = (f32[8,8,512]{2,1,0:T(8,128)S(1)}, f32[8,8,512]{2,1,0:T(8,128)S(1)}, u32[]{:S(2)}, u32[]{:S(2)}) collective-permute-start(f32[8,8,512]{2,1,0:T(8,128)S(1)} %add.889), channel_id=1, source_target_pairs={{0,4},{4,8},{8,12},{12,16},{16,20},{20,24},{24,28},{1,5},{5,9},{9,... | collective-permute-start | bytes 393224 | tf_op jit(solution)/shard_map/ppermute | solution.py:31
  146.3 4.1 %collective-permute-start.7 = (f32[3,2,8,512]{3,2,1,0:T(8,128)S(1)}, f32[3,2,8,512]{3,2,1,0:T(8,128)S(1)}, u32[]{:S(2)}, u32[]{:S(2)}) collective-permute-start(f32[3,2,8,512]{3,2,1,0:T(8,128)S(1)} %get-tuple-element.521), channel_id=1, source_target_pairs={{0,1},{1,2},{2,3},{3,0},{4,5},{5,6},{6,7},{7,4},{8,9},{9,10},{10,1... | collective-permute-start | bytes 294920 | tf_op jit(solution)/shard_map/ppermute | solution.py:22
  146.4 4.1 %collective-permute-start.8 = (f32[3,2,8,512]{3,2,1,0:T(8,128)S(1)}, f32[3,2,8,512]{3,2,1,0:T(8,128)S(1)}, u32[]{:S(2)}, u32[]{:S(2)}) collective-permute-start(f32[3,2,8,512]{3,2,1,0:T(8,128)S(1)} %get-tuple-element.522), channel_id=1, source_target_pairs={{1,0},{2,1},{3,2},{0,3},{5,4},{6,5},{7,6},{4,7},{9,8},{10,9},{11,1... | collective-permute-start | bytes 294920 | tf_op jit(solution)/shard_map/ppermute | solution.py:23
  152.9 3.6 %collective-permute-start.10 = (f32[1,2,8,512]{3,2,1,0:T(8,128)S(1)}, f32[1,2,8,512]{3,2,1,0:T(8,128)S(1)}, u32[]{:S(2)}, u32[]{:S(2)}) collective-permute-start(f32[1,2,8,512]{3,2,1,0:T(8,128)S(1)} %get-tuple-element.586), channel_id=1, source_target_pairs={{1,0},{2,1},{3,2},{0,3},{5,4},{6,5},{7,6},{4,7},{9,8},{10,9},{11,1... | collective-permute-start | bytes 98312 | tf_op jit(solution)/shard_map/ppermute | solution.py:23
  154.9 3.5 %collective-permute-start.9 = (f32[1,2,8,512]{3,2,1,0:T(8,128)S(1)}, f32[1,2,8,512]{3,2,1,0:T(8,128)S(1)}, u32[]{:S(2)}, u32[]{:S(2)}) collective-permute-start(f32[1,2,8,512]{3,2,1,0:T(8,128)S(1)} %get-tuple-element.585), channel_id=1, source_target_pairs={{0,1},{1,2},{2,3},{3,0},{4,5},{5,6},{6,7},{7,4},{8,9},{9,10},{10,1... | collective-permute-start | bytes 98312 | tf_op jit(solution)/shard_map/ppermute | solution.py:22
  159.6 15.7 %collective-permute-start.11 = (f32[1,2,8,512]{3,2,1,0:T(8,128)S(1)}, f32[1,2,8,512]{3,2,1,0:T(8,128)S(1)}, u32[]{:S(2)}, u32[]{:S(2)}) collective-permute-start(f32[1,2,8,512]{3,2,1,0:T(8,128)S(1)} %get-tuple-element.583), channel_id=1, source_target_pairs={{0,1},{1,2},{2,3},{3,0},{4,5},{5,6},{6,7},{7,4},{8,9},{9,10},{10,1... | collective-permute-start | bytes 98312 | tf_op jit(solution)/shard_map/ppermute | solution.py:22
  159.7 15.6 %collective-permute-start.12 = (f32[1,2,8,512]{3,2,1,0:T(8,128)S(1)}, f32[1,2,8,512]{3,2,1,0:T(8,128)S(1)}, u32[]{:S(2)}, u32[]{:S(2)}) collective-permute-start(f32[1,2,8,512]{3,2,1,0:T(8,128)S(1)} %get-tuple-element.584), channel_id=1, source_target_pairs={{1,0},{2,1},{3,2},{0,3},{5,4},{6,5},{7,6},{4,7},{9,8},{10,9},{11,1... | collective-permute-start | bytes 98312 | tf_op jit(solution)/shard_map/ppermute | solution.py:23
  176.4 44.5 %copy-start.1 = (f32[4,4,256]{2,1,0:T(4,128)S(1)}, f32[4,4,256]{2,1,0:T(4,128)}, u32[]{:S(2)}) copy-start(f32[4,4,256]{2,1,0:T(4,128)} %copy-done) | copy-start | bytes 49156
where the time goes:
time: 239 us; the launch traced here: 238 us
  local copies, waits for them, and re-layouts  113 us (47%)
  blocking collectives  61.8 us (26%)
  other arithmetic  38.3 us (16%)
  starting transfers between devices  15.6 us (7%)
  waiting for transfers between devices  7.47 us (3%)
    reshape x7, local copies, waits for them, and re-layouts, restrict(): values.reshape(leading + (plane_count // 2, 2, row_count // 2, 2, col_cou...  69.2 us
    all_gather x2, blocking collectives, on_device(): all_forcing = lax.all_gather(forcing[None], 'tm', axis=0, tiled=True)  61.8 us
    reduce_sum x7, other arithmetic, restrict(): return jnp.sum(blocks, axis=(-5, -3, -1)) * 0.125  28.2 us
    reshape x3, local copies, waits for them, and re-layouts, prolong(): spread.reshape(leading + (2 * plane_count, 2 * row_count, 2 * col_count))  20.8 us
    broadcast_in_dim x3, local copies, waits for them, and re-layouts, prolong(): jnp.broadcast_to(coarse[..., :, None, :, None, :, None], leading + (plane...  11.7 us
    ppermute x6, starting transfers between devices, with_halo(): after = lax.ppermute(leading, axis, down)  8.53 us
    ppermute x6, waiting for transfers between devices, with_halo(): before = lax.ppermute(last, axis, up)  5.7 us
  transfers between devices with their start and end apart: 13, of which 6 were waited for; matrix products, arithmetic and copies ran while one was open for 28% of the time, Pallas kernels for 0%

commit v1 on v0

v1 whole, which is shorter than its diff:
```python
import functools

import jax
import jax.numpy as jnp
from jax import lax
from jax.experimental import pallas as pl
from jax.experimental.pallas import tpu as pltpu
from jax.sharding import PartitionSpec as P


DT = 0.016
HALO = 12
MESH = pl.DeviceIdType.MESH


def roll(x, shift, axis):
    return pltpu.roll(x, shift % x.shape[axis], axis)


def chem_mob(below, here, above, coef):
    square = here * here
    around = (
        (below + above)
        + (roll(here, 1, 0) + roll(here, -1, 0))
        + (roll(here, 1, 1) + roll(here, -1, 1))
    )
    chem = here * (square + 5.0) - around
    mob = coef * jnp.maximum(1.0 - square, 0.0)
    return chem, mob


def sweep(src, coef, lo, hi, emit):
    chem_lo, mob_lo = chem_mob(src[lo - 2], src[lo - 1], src[lo], coef[lo - 1])
    here, above = src[lo], src[lo + 1]
    chem, mob = chem_mob(src[lo - 1], here, above, coef[lo])
    flux = (mob_lo + mob) * (chem - chem_lo)

    def step(i, state):
        for j in range(2):
            here, above, chem, mob, flux = state
            k = lo + 2 * i + j
            top = src[k + 2]
            chem_up, mob_up = chem_mob(here, above, top, coef[k + 1])
            flux_up = (mob + mob_up) * (chem_up - chem)
            fy = (roll(mob, -1, 0) + mob) * (roll(chem, -1, 0) - chem)
            fx = (roll(mob, -1, 1) + mob) * (roll(chem, -1, 1) - chem)
            total = (flux_up - flux) + (fy - roll(fy, 1, 0)) + (fx - roll(fx, 1, 1))
            emit(k, here, 0.5 * total)
            state = (above, top, chem_up, mob_up, flux_up)
        return state

    lax.fori_loop(0, (hi - lo) // 2, step, (here, above, chem, mob, flux))


def parities(shape):
    rows = lax.broadcasted_iota(jnp.int32, shape, 0)
    cols = lax.broadcasted_iota(jnp.int32, shape, 1)
    return rows % 2 == 0, cols % 2 == 0


def pair(even, a, b, axis):
    kept = jnp.where(even, a, b)
    moved = jnp.where(even, b, a)
    return kept + jnp.where(even, roll(moved, -1, axis), roll(moved, 1, axis))


def pack(src, planes, even_row, even_col):
    sums = [src[2 * q] + src[2 * q + 1] for q in planes]
    upper = pair(even_col, sums[0], sums[1], 1)
    lower = pair(even_col, sums[2], sums[3], 1)
    return 0.125 * pair(even_row, upper, lower, 0)


def unpack(packed, even_row, even_col):
    by_col = (
        jnp.where(even_col, packed, roll(packed, 1, 1)),
        jnp.where(even_col, roll(packed, -1, 1), packed),
    )
    out = []
    for x in by_col:
        out.append(jnp.where(even_row, x, roll(x, 1, 0)))
    for x in by_col:
        out.append(jnp.where(even_row, roll(x, -1, 0), x))
    return out


def coarse_flow(w, coef):
    square = w * w
    around = (roll(w, 2, 0) + roll(w, -2, 0)) + (roll(w, 2, 1) + roll(w, -2, 1))
    chem = w * square - 0.25 * around
    mob = coef * jnp.maximum(1.0 - square, 0.0)
    fy = (roll(mob, -2, 0) + mob) * (roll(chem, -2, 0) - chem)
    fx = (roll(mob, -2, 1) + mob) * (roll(chem, -2, 1) - chem)
    return 0.125 * ((fy - roll(fy, 2, 0)) + (fx - roll(fx, 2, 1)))


def kernel(
    n_tm, n_sp, u_hbm, c_hbm, out, u, c, quad, mid, end, start, node1, node2, mid2, rest,
    forcings, near_send, near_recv, far_send, far_recv, own_sem, tm_send, tm_recv,
):
    planes = u_hbm.shape[0]
    far = HALO - planes
    own = HALO
    t = lax.axis_index("tm")
    s = lax.axis_index("space")
    up, down = lax.rem(s + 1, n_sp), lax.rem(s + n_sp - 1, n_sp)
    up2, down2 = lax.rem(s + 2, n_sp), lax.rem(s + n_sp - 2, n_sp)
    odd = lax.rem(s, 2)
    mate = s + 1 - 2 * odd
    forward = n_sp == 4

    barrier = pltpu.get_barrier_semaphore()
    peers = (up, down) if forward else (up, down, up2, down2)
    for peer in peers:
        pl.semaphore_signal(barrier, inc=1, device_id={"space": peer}, device_id_type=MESH)

    def greet(d, carry):
        pl.semaphore_signal(
            barrier, inc=1, device_id={"tm": lax.rem(t + d, n_tm)}, device_id_type=MESH
        )
        return carry

    lax.fori_loop(1, n_tm, greet, 0)

    local = [
        pltpu.make_async_copy(src, dst.at[pl.ds(own, planes)], own_sem.at[i])
        for i, (src, dst) in enumerate(((u_hbm, u), (c_hbm, c)))
    ]
    for copy in local:
        copy.start()
    pl.semaphore_wait(barrier, len(peers) + n_tm - 1)

    def remote(src, dst, send, recv, peer):
        return pltpu.make_async_remote_copy(
            src_ref=src, dst_ref=dst, send_sem=send, recv_sem=recv,
            device_id={"space": peer}, device_id_type=MESH,
        )

    near = []
    for f, (src, dst) in enumerate(((u_hbm, u), (c_hbm, c))):
        near.append((
            remote(src, dst.at[pl.ds(far, planes)], near_send.at[f, 0], near_recv.at[f, 0], up),
            remote(src, dst.at[pl.ds(own + planes, planes)], near_send.at[f, 1], near_recv.at[f, 1], down),
        ))
        for copy in near[f]:
            copy.start()
    far_copies = []
    if forward:
        cross = odd
        base = far + odd * (own + planes - far)
        for f, dst in enumerate((u, c)):
            remote(
                dst.at[pl.ds(far, planes)], dst.at[pl.ds(far, planes)],
                near_send.at[f, 0], near_recv.at[f, cross], mate,
            ).wait_recv()
            lows = dst.at[pl.ds(base + planes - far, far)]
            highs = dst.at[pl.ds(base, far)]
            for side, (src, at) in enumerate(((lows, 0), (highs, own + 2 * planes))):
                copy = remote(src, dst.at[pl.ds(at, far)], far_send.at[f, side], far_recv.at[f, side], mate)
                copy.start()
                far_copies.append(copy)
        for f, dst in enumerate((u, c)):
            remote(
                dst.at[pl.ds(far, planes)], dst.at[pl.ds(far, planes)],
                near_send.at[f, 0], near_recv.at[f, 1 - cross], mate,
            ).wait_recv()
    else:
        for f, (src, dst) in enumerate(((u_hbm, u), (c_hbm, c))):
            lows = src.at[pl.ds(planes - far, far)]
            highs = src.at[pl.ds(0, far)]
            far_copies.append(remote(lows, dst.at[pl.ds(0, far)], far_send.at[f, 0], far_recv.at[f, 0], up2))
            far_copies.append(remote(highs, dst.at[pl.ds(own + 2 * planes, far)], far_send.at[f, 1], far_recv.at[f, 1], down2))
        for copy in far_copies:
            copy.start()
        for f in range(2):
            for copy in near[f]:
                copy.wait_recv()
    for copy in far_copies:
        copy.wait()
    for f in range(2):
        for copy in near[f]:
            copy.wait_send()
    for copy in local:
        copy.wait()

    total = planes + 2 * HALO
    even_row, even_col = parities(u.shape[1:])

    def emit_mid(k, v, force):
        quad[k] = force
        mid[k] = v + (0.5 * DT) * force

    sweep(u, c, 2, total - 2, emit_mid)

    def emit_end(k, v, force):
        quad[k] = quad[k] + 4.0 * force
        end[k] = v + (0.5 * DT) * force

    sweep(mid, c, 4, total - 4, emit_end)

    def emit_quad(k, v, force):
        quad[k] = quad[k] + force

    sweep(end, c, 6, total - 6, emit_quad)

    mine = list(range(own // 2, (own + planes) // 2))
    others = [q for q in range(3, (total - 6) // 2) if q not in mine]
    groups = []
    for part in (mine, others):
        for i in range(0, len(part), 4):
            group = part[i : i + 4]
            groups.append((group + group + group + group)[:4])
    own_groups = -(-len(mine) // 4)

    coefs = [pack(c, g, even_row, even_col) for g in groups]
    v0 = [pack(u, g, even_row, even_col) for g in groups]
    v1 = [pack(end, g, even_row, even_col) for g in groups]
    force0 = [
        (DT / 6.0) * pack(quad, g, even_row, even_col) - DT * coarse_flow(v, m)
        for g, v, m in zip(groups, v0, coefs)
    ]

    def advance(p, state):
        return tuple(
            w + DT * coarse_flow(w, m) + f for w, m, f in zip(state, coefs, force0)
        )

    w0 = lax.fori_loop(0, t, advance, tuple(v0))
    w1 = advance(0, w0)
    first = t == 0
    for i, g in enumerate(groups):
        by_start = unpack(w0[i] - v1[i], even_row, even_col)
        by_mid = unpack(0.5 * ((w0[i] - v0[i]) + (w1[i] - v1[i])), even_row, even_col)
        by_end = unpack(w1[i] - v1[i], even_row, even_col)
        for j, q in enumerate(g):
            if q in g[:j]:
                continue
            for k in (2 * q, 2 * q + 1):
                start[k] = jnp.where(first, u[k], end[k] + by_start[j])
                node1[k] = mid[k] + by_mid[j]
                node2[k] = end[k] + by_end[j]

    def emit_f0(k, v, force):
        quad[k] = force
        mid2[k] = v + (DT * 5.0 / 24.0) * force
        rest[k] = (-DT / 24.0) * force

    sweep(start, c, 8, total - 8, emit_f0)

    def emit_f1(k, v, force):
        mid2[k] = mid2[k] + (DT / 3.0) * force
        rest[k] = rest[k] - (DT / 6.0) * force

    sweep(node1, c, 8, total - 8, emit_f1)

    def emit_f2(k, v, force):
        mid2[k] = mid2[k] - (DT / 24.0) * force
        rest[k] = rest[k] + (DT * 5.0 / 24.0) * force

    sweep(node2, c, 8, total - 8, emit_f2)

    def emit_end2(k, v, force):
        quad[k] = quad[k] + 4.0 * force
        end[k] = v + (0.5 * DT) * force + rest[k]

    sweep(mid2, c, 10, total - 10, emit_end2)
    sweep(end, c, 12, total - 12, emit_quad)

    for i in range(own_groups):
        g = groups[i]
        before = pack(start, g, even_row, even_col)
        forcings[t, i] = (DT / 6.0) * pack(quad, g, even_row, even_col) - DT * coarse_flow(before, coefs[i])

    def to_slice(d):
        return pltpu.make_async_remote_copy(
            src_ref=forcings.at[t], dst_ref=forcings.at[t],
            send_sem=tm_send.at[d], recv_sem=tm_recv.at[t],
            device_id={"tm": lax.rem(t + d, n_tm)}, device_id_type=MESH,
        )

    def send(i, carry):
        d = n_tm - 1 - i

        @pl.when(t + d < n_tm)
        def _():
            to_slice(d).start()

        return carry

    lax.fori_loop(0, n_tm - 1, send, 0)

    last = [pack(end, g, even_row, even_col) for g in groups[:own_groups]]

    def follow(p, state):
        pltpu.make_async_remote_copy(
            src_ref=forcings.at[p], dst_ref=forcings.at[p],
            send_sem=tm_send.at[0], recv_sem=tm_recv.at[p],
            device_id={"tm": lax.rem(t + 1, n_tm)}, device_id_type=MESH,
        ).wait_recv()
        return tuple(
            w + DT * coarse_flow(w, coefs[i]) + forcings[p, i] for i, w in enumerate(state)
        )

    state = lax.fori_loop(0, t, follow, tuple(v0[:own_groups]))
    for i in range(own_groups):
        w = state[i] + DT * coarse_flow(state[i], coefs[i]) + forcings[t, i]
        fixes = unpack(w - last[i], even_row, even_col)
        for j, q in enumerate(groups[i]):
            for k in (2 * q, 2 * q + 1):
                out[k - own] = end[k] + fixes[j]

    def sent(d, carry):
        @pl.when(t + d < n_tm)
        def _():
            to_slice(d).wait_send()

        return carry

    lax.fori_loop(1, n_tm, sent, 0)


def solution(mesh):
    n_tm, n_sp = mesh.shape["tm"], mesh.shape["space"]

    def on_device(initial_field, mobility):
        planes, rows, cols = initial_field.shape
        wide = pltpu.VMEM((planes + 2 * HALO, rows, cols), jnp.float32)
        out = pl.pallas_call(
            functools.partial(kernel, n_tm, n_sp),
            out_shape=jax.ShapeDtypeStruct(initial_field.shape, jnp.float32),
            in_specs=[pl.BlockSpec(memory_space=pl.ANY)] * 2,
            out_specs=pl.BlockSpec(memory_space=pltpu.VMEM),
            scratch_shapes=[wide] * 10
            + [
                pltpu.VMEM((n_tm, -(-planes // 8), rows, cols), jnp.float32),
                pltpu.SemaphoreType.DMA((2, 2)),
                pltpu.SemaphoreType.DMA((2, 2)),
                pltpu.SemaphoreType.DMA((2, 2)),
                pltpu.SemaphoreType.DMA((2, 2)),
                pltpu.SemaphoreType.DMA((2,)),
                pltpu.SemaphoreType.DMA((n_tm,)),
                pltpu.SemaphoreType.DMA((n_tm,)),
            ],
            compiler_params=pltpu.CompilerParams(
                collective_id=0, has_side_effects=True, vmem_limit_bytes=32 * 2**20
            ),
        )(initial_field, mobility)
        return out[None]

    specs = (P("space", None, None), P("space", None, None))
    return jax.shard_map(
        on_device, mesh=mesh, in_specs=specs, out_specs=P("tm", "space", None, None), check_vma=False
    )
```

time: 239 us -> 37.6 us (0.16)
  the two profiles are of different devices: /device:TPU:0 before, /device:TPU:17 now
where the time goes in v1:
time: 37.6 us; the launch traced here: 37.3 us
  Pallas kernels  34.8 us (93%)
  local copies, waits for them, and re-layouts  2.47 us (7%)
    pallas_call x1, Pallas kernels, on_device(): pl.pallas_call(functools.partial(kernel, n_tm, n_sp), out_shape=jax.Shape...  34.8 us
    unnamed x5, local copies, waits for them, and re-layouts  2.47 us

profile of v1, /device:TPU:17, one launch (start us, length us, event | category | flops | bytes accessed | tf_op | source)
XLA Modules:
  0.0 37.3 jit_solution(14180956993506225589)
XLA Ops:
  0.0 0.0 copy-start
  0.0 0.9 %copy-done = f32[8,8,512]{2,1,0:T(8,128)S(1)} copy-done((f32[8,8,512]{2,1,0:T(8,128)S(1)}, f32[8,8,512]{2,1,0:T(8,128)}, u32[]{:S(2)}) %copy-start) | copy-done | bytes 131096
  0.9 0.0 copy-start.1
  0.9 0.9 %copy-done.1 = f32[8,8,512]{2,1,0:T(8,128)S(1)} copy-done((f32[8,8,512]{2,1,0:T(8,128)S(1)}, f32[8,8,512]{2,1,0:T(8,128)}, u32[]{:S(2)}) %copy-start.1) | copy-done | bytes 131096
  1.8 34.8 %shard_map.28 = f32[8,8,512]{2,1,0:T(8,128)S(1)} custom-call(f32[8,8,512]{2,1,0:T(8,128)S(1)} %copy-done, f32[8,8,512]{2,1,0:T(8,128)S(1)} %copy-done.1), custom_call_target="tpu_custom_call" | custom-call | tf_op jit(solution)/shard_map/pallas_call | solution.py:328
  36.6 0.7 %copy.4 = f32[1,8,8,512]{3,2,1,0:T(8,128)} copy(f32[1,8,8,512]{3,2,1,0:T(8,128)S(1)} %bitcast.1) | data formatting | bytes 262144
Async XLA Ops:
  0.0 0.9 %copy-start = (f32[8,8,512]{2,1,0:T(8,128)S(1)}, f32[8,8,512]{2,1,0:T(8,128)}, u32[]{:S(2)}) copy-start(f32[8,8,512]{2,1,0:T(8,128)} %u_hbm.1) | copy-start | bytes 393220
  0.9 0.9 %copy-start.1 = (f32[8,8,512]{2,1,0:T(8,128)S(1)}, f32[8,8,512]{2,1,0:T(8,128)}, u32[]{:S(2)}) copy-start(f32[8,8,512]{2,1,0:T(8,128)} %c_hbm.1) | copy-start | bytes 393220

commit v2 on v1

--- a/solution.py
+++ b/solution.py
@@ -15,6 +15,14 @@
 
 def roll(x, shift, axis):
     return pltpu.roll(x, shift % x.shape[axis], axis)
+
+
+class Mirrored:
+    def __init__(self, ref, origin, sign):
+        self.ref, self.origin, self.sign = ref, origin, sign
+
+    def __getitem__(self, k):
+        return self.ref[self.origin + self.sign * k]
 
 
 def chem_mob(below, here, above, coef):
@@ -36,9 +44,9 @@
     flux = (mob_lo + mob) * (chem - chem_lo)
 
     def step(i, state):
-        for j in range(2):
+        for j in range(4):
             here, above, chem, mob, flux = state
-            k = lo + 2 * i + j
+            k = lo + 4 * i + j
             top = src[k + 2]
             chem_up, mob_up = chem_mob(here, above, top, coef[k + 1])
             flux_up = (mob + mob_up) * (chem_up - chem)
@@ -49,7 +57,7 @@
             state = (above, top, chem_up, mob_up, flux_up)
         return state
 
-    lax.fori_loop(0, (hi - lo) // 2, step, (here, above, chem, mob, flux))
+    lax.fori_loop(0, (hi - lo) // 4, step, (here, above, chem, mob, flux))
 
 
 def parities(shape):
@@ -96,7 +104,7 @@
 
 def kernel(
     n_tm, n_sp, u_hbm, c_hbm, out, u, c, quad, mid, end, start, node1, node2, mid2, rest,
-    forcings, near_send, near_recv, far_send, far_recv, own_sem, tm_send, tm_recv,
+    forcings, sp_send, sp_recv, own_sem, tm_send, tm_recv,
 ):
     planes = u_hbm.shape[0]
     far = HALO - planes
@@ -130,78 +138,84 @@
         copy.start()
     pl.semaphore_wait(barrier, len(peers) + n_tm - 1)
 
-    def remote(src, dst, send, recv, peer):
+    def remote(f, kind, src, src_at, dst_at, rows, peer):
         return pltpu.make_async_remote_copy(
-            src_ref=src, dst_ref=dst, send_sem=send, recv_sem=recv,
+            src_ref=src.at[pl.ds(src_at, rows)], dst_ref=(u, c)[f].at[pl.ds(dst_at, rows)],
+            send_sem=sp_send.at[f, kind], recv_sem=sp_recv.at[f, kind],
             device_id={"space": peer}, device_id_type=MESH,
         )
 
-    near = []
-    for f, (src, dst) in enumerate(((u_hbm, u), (c_hbm, c))):
-        near.append((
-            remote(src, dst.at[pl.ds(far, planes)], near_send.at[f, 0], near_recv.at[f, 0], up),
-            remote(src, dst.at[pl.ds(own + planes, planes)], near_send.at[f, 1], near_recv.at[f, 1], down),
-        ))
-        for copy in near[f]:
+    def pick(even, other):
+        return even + odd * (other - even)
+
+    half = planes // 2
+    lower, upper = own - planes, own + planes
+    inputs = (u_hbm, c_hbm)
+    cross = pick(down, up)
+    mates, nears, fars, mate_nears, mate_fars = [], [], [], [], []
+    for f in range(2):
+        nears.append(remote(f, 1, inputs[f], pick(0, half), pick(upper, own - half), half, cross))
+    for f in range(2):
+        mates.append(remote(f, 0, inputs[f], 0, pick(lower, upper), planes, mate))
+    for f in range(2):
+        fars.append(remote(f, 2, inputs[f], pick(half, 0), pick(upper + half, lower), half, cross))
+    for f in range(2):
+        if forward:
+            mate_nears.append(remote(f, 3, (u, c)[f], pick(own - half, upper), pick(0, upper + planes), far, mate))
+            mate_fars.append(remote(f, 4, (u, c)[f], pick(lower, upper + half), pick(upper + planes, 0), far, mate))
+        else:
+            mate_nears.append(remote(f, 3, inputs[f], pick(0, planes - far), pick(upper + planes, 0), far, pick(down2, up2)))
+            mate_fars.append(remote(f, 4, inputs[f], pick(planes - far, 0), pick(0, upper + planes), far, pick(up2, down2)))
+    for copy in nears + mates + fars:
+        copy.start()
+    if not forward:
+        for copy in mate_nears + mate_fars:
             copy.start()
-    far_copies = []
-    if forward:
-        cross = odd
-        base = far + odd * (own + planes - far)
-        for f, dst in enumerate((u, c)):
-            remote(
-                dst.at[pl.ds(far, planes)], dst.at[pl.ds(far, planes)],
-                near_send.at[f, 0], near_recv.at[f, cross], mate,
-            ).wait_recv()
-            lows = dst.at[pl.ds(base + planes - far, far)]
-            highs = dst.at[pl.ds(base, far)]
-            for side, (src, at) in enumerate(((lows, 0), (highs, own + 2 * planes))):
-                copy = remote(src, dst.at[pl.ds(at, far)], far_send.at[f, side], far_recv.at[f, side], mate)
-                copy.start()
-                far_copies.append(copy)
-        for f, dst in enumerate((u, c)):
-            remote(
-                dst.at[pl.ds(far, planes)], dst.at[pl.ds(far, planes)],
-                near_send.at[f, 0], near_recv.at[f, 1 - cross], mate,
-            ).wait_recv()
-    else:
-        for f, (src, dst) in enumerate(((u_hbm, u), (c_hbm, c))):
-            lows = src.at[pl.ds(planes - far, far)]
-            highs = src.at[pl.ds(0, far)]
-            far_copies.append(remote(lows, dst.at[pl.ds(0, far)], far_send.at[f, 0], far_recv.at[f, 0], up2))
-            far_copies.append(remote(highs, dst.at[pl.ds(own + 2 * planes, far)], far_send.at[f, 1], far_recv.at[f, 1], down2))
-        for copy in far_copies:
-            copy.start()
-        for f in range(2):
-            for copy in near[f]:
-                copy.wait_recv()
-    for copy in far_copies:
-        copy.wait()
-    for f in range(2):
-        for copy in near[f]:
-            copy.wait_send()
-    for copy in local:
-        copy.wait()
 
     total = planes + 2 * HALO
     even_row, even_col = parities(u.shape[1:])
+    origin, sign = odd * (total - 1), 1 - 2 * odd
+    ui, ci = Mirrored(u, origin, sign), Mirrored(c, origin, sign)
 
     def emit_mid(k, v, force):
         quad[k] = force
         mid[k] = v + (0.5 * DT) * force
 
-    sweep(u, c, 2, total - 2, emit_mid)
-
     def emit_end(k, v, force):
         quad[k] = quad[k] + 4.0 * force
         end[k] = v + (0.5 * DT) * force
 
-    sweep(mid, c, 4, total - 4, emit_end)
-
     def emit_quad(k, v, force):
         quad[k] = quad[k] + force
 
-    sweep(end, c, 6, total - 6, emit_quad)
+    for copy in local:
+        copy.wait()
+    for copy in mates:
+        copy.wait_recv()
+    top = own + 2 * planes
+    sweep(ui, ci, own + 2, top - 2, emit_mid)
+    sweep(mid, ci, own + 4, top - 4, emit_end)
+    sweep(end, ci, own + 6, top - 6, emit_quad)
+
+    for arrived, passed in ((nears, mate_nears), (fars, mate_fars)):
+        for i in range(2):
+            arrived[i].wait_recv()
+            if forward:
+                passed[i].start()
+        for copy in passed:
+            copy.wait_recv()
+        if arrived is nears:
+            low = own - half
+            sweep(ui, ci, low + 2, own + 2, emit_mid)
+            sweep(ui, ci, top - 2, top + 2, emit_mid)
+            sweep(mid, ci, low + 4, own + 4, emit_end)
+            sweep(mid, ci, top - 4, top, emit_end)
+            sweep(end, ci, low + 6, own + 6, emit_quad)
+            sweep(end, ci, top - 6, top - 2, emit_quad)
+        else:
+            sweep(ui, ci, 2, low + 2, emit_mid)
+            sweep(mid, ci, 4, low + 4, emit_end)
+            sweep(end, ci, 6, low + 6, emit_quad)
 
     mine = list(range(own // 2, (own + planes) // 2))
     others = [q for q in range(3, (total - 6) // 2) if q not in mine]
@@ -212,8 +226,8 @@
             groups.append((group + group + group + group)[:4])
     own_groups = -(-len(mine) // 4)
 
-    coefs = [pack(c, g, even_row, even_col) for g in groups]
-    v0 = [pack(u, g, even_row, even_col) for g in groups]
+    coefs = [pack(ci, g, even_row, even_col) for g in groups]
+    v0 = [pack(ui, g, even_row, even_col) for g in groups]
     v1 = [pack(end, g, even_row, even_col) for g in groups]
     force0 = [
         (DT / 6.0) * pack(quad, g, even_row, even_col) - DT * coarse_flow(v, m)
@@ -236,7 +250,7 @@
             if q in g[:j]:
                 continue
             for k in (2 * q, 2 * q + 1):
-                start[k] = jnp.where(first, u[k], end[k] + by_start[j])
+                start[k] = jnp.where(first, ui[k], end[k] + by_start[j])
                 node1[k] = mid[k] + by_mid[j]
                 node2[k] = end[k] + by_end[j]
 
@@ -245,26 +259,26 @@
         mid2[k] = v + (DT * 5.0 / 24.0) * force
         rest[k] = (-DT / 24.0) * force
 
-    sweep(start, c, 8, total - 8, emit_f0)
+    sweep(start, ci, 8, total - 8, emit_f0)
 
     def emit_f1(k, v, force):
         mid2[k] = mid2[k] + (DT / 3.0) * force
         rest[k] = rest[k] - (DT / 6.0) * force
 
-    sweep(node1, c, 8, total - 8, emit_f1)
+    sweep(node1, ci, 8, total - 8, emit_f1)
 
     def emit_f2(k, v, force):
         mid2[k] = mid2[k] - (DT / 24.0) * force
         rest[k] = rest[k] + (DT * 5.0 / 24.0) * force
 
-    sweep(node2, c, 8, total - 8, emit_f2)
+    sweep(node2, ci, 8, total - 8, emit_f2)
 
     def emit_end2(k, v, force):
         quad[k] = quad[k] + 4.0 * force
         end[k] = v + (0.5 * DT) * force + rest[k]
 
-    sweep(mid2, c, 10, total - 10, emit_end2)
-    sweep(end, c, 12, total - 12, emit_quad)
+    sweep(mid2, ci, 10, total - 10, emit_end2)
+    sweep(end, ci, 12, total - 12, emit_quad)
 
     for i in range(own_groups):
         g = groups[i]
@@ -307,7 +321,7 @@
         fixes = unpack(w - last[i], even_row, even_col)
         for j, q in enumerate(groups[i]):
             for k in (2 * q, 2 * q + 1):
-                out[k - own] = end[k] + fixes[j]
+                out[origin + sign * k - own] = end[k] + fixes[j]
 
     def sent(d, carry):
         @pl.when(t + d < n_tm)
@@ -317,6 +331,8 @@
         return carry
 
     lax.fori_loop(1, n_tm, sent, 0)
+    for copy in nears + mates + fars + mate_nears + mate_fars:
+        copy.wait_send()
 
 
 def solution(mesh):
@@ -333,10 +349,8 @@
             scratch_shapes=[wide] * 10
             + [
                 pltpu.VMEM((n_tm, -(-planes // 8), rows, cols), jnp.float32),
-                pltpu.SemaphoreType.DMA((2, 2)),
-                pltpu.SemaphoreType.DMA((2, 2)),
-                pltpu.SemaphoreType.DMA((2, 2)),
-                pltpu.SemaphoreType.DMA((2, 2)),
+                pltpu.SemaphoreType.DMA((2, 5)),
+                pltpu.SemaphoreType.DMA((2, 5)),
                 pltpu.SemaphoreType.DMA((2,)),
                 pltpu.SemaphoreType.DMA((n_tm,)),
                 pltpu.SemaphoreType.DMA((n_tm,)),

time: 37.6 us -> 28.4 us (0.76)
  Pallas kernels: 34.8 us -> 25.8 us
    pallas_call x1, Pallas kernels: 34.8 us -> 25.8 us  [on_device(): pl.pallas_call(functools.partial(kernel, n_tm, n_sp), out_shape=jax.Shape...]
where the time goes in v2:
time: 28.4 us; the launch traced here: 28.3 us
  Pallas kernels  25.8 us (91%)
  local copies, waits for them, and re-layouts  2.47 us (9%)
    pallas_call x1, Pallas kernels, on_device(): pl.pallas_call(functools.partial(kernel, n_tm, n_sp), out_shape=jax.Shape...  25.8 us
    unnamed x5, local copies, waits for them, and re-layouts  2.47 us

profile of v2, /device:TPU:17, one launch (start us, length us, event | category | flops | bytes accessed | tf_op | source)
XLA Modules:
  0.0 28.3 jit_solution(6995159534435124962)
XLA Ops:
  0.0 0.0 copy-start
  0.0 0.9 %copy-done = f32[8,8,512]{2,1,0:T(8,128)S(1)} copy-done((f32[8,8,512]{2,1,0:T(8,128)S(1)}, f32[8,8,512]{2,1,0:T(8,128)}, u32[]{:S(2)}) %copy-start) | copy-done | bytes 131096
  0.9 0.0 copy-start.1
  0.9 0.9 %copy-done.1 = f32[8,8,512]{2,1,0:T(8,128)S(1)} copy-done((f32[8,8,512]{2,1,0:T(8,128)S(1)}, f32[8,8,512]{2,1,0:T(8,128)}, u32[]{:S(2)}) %copy-start.1) | copy-done | bytes 131096
  1.8 25.8 %shard_map.28 = f32[8,8,512]{2,1,0:T(8,128)S(1)} custom-call(f32[8,8,512]{2,1,0:T(8,128)S(1)} %copy-done, f32[8,8,512]{2,1,0:T(8,128)S(1)} %copy-done.1), custom_call_target="tpu_custom_call" | custom-call | tf_op jit(solution)/shard_map/pallas_call | solution.py:344
  27.6 0.7 %copy.4 = f32[1,8,8,512]{3,2,1,0:T(8,128)} copy(f32[1,8,8,512]{3,2,1,0:T(8,128)S(1)} %bitcast.1) | data formatting | bytes 262144
Async XLA Ops:
  0.0 0.9 %copy-start = (f32[8,8,512]{2,1,0:T(8,128)S(1)}, f32[8,8,512]{2,1,0:T(8,128)}, u32[]{:S(2)}) copy-start(f32[8,8,512]{2,1,0:T(8,128)} %u_hbm.1) | copy-start | bytes 393220
  0.9 0.9 %copy-start.1 = (f32[8,8,512]{2,1,0:T(8,128)S(1)}, f32[8,8,512]{2,1,0:T(8,128)}, u32[]{:S(2)}) copy-start(f32[8,8,512]{2,1,0:T(8,128)} %c_hbm.1) | copy-start | bytes 393220

commit v3 on v2

--- a/solution.py
+++ b/solution.py
@@ -37,27 +37,36 @@
     return chem, mob
 
 
-def sweep(src, coef, lo, hi, emit):
-    chem_lo, mob_lo = chem_mob(src[lo - 2], src[lo - 1], src[lo], coef[lo - 1])
-    here, above = src[lo], src[lo + 1]
-    chem, mob = chem_mob(src[lo - 1], here, above, coef[lo])
-    flux = (mob_lo + mob) * (chem - chem_lo)
-
-    def step(i, state):
-        for j in range(4):
-            here, above, chem, mob, flux = state
-            k = lo + 4 * i + j
-            top = src[k + 2]
-            chem_up, mob_up = chem_mob(here, above, top, coef[k + 1])
-            flux_up = (mob + mob_up) * (chem_up - chem)
-            fy = (roll(mob, -1, 0) + mob) * (roll(chem, -1, 0) - chem)
-            fx = (roll(mob, -1, 1) + mob) * (roll(chem, -1, 1) - chem)
-            total = (flux_up - flux) + (fy - roll(fy, 1, 0)) + (fx - roll(fx, 1, 1))
-            emit(k, here, 0.5 * total)
-            state = (above, top, chem_up, mob_up, flux_up)
-        return state
-
-    lax.fori_loop(0, (hi - lo) // 4, step, (here, above, chem, mob, flux))
+def sweep(sources, coef, lo, hi, emit, steps=0):
+    steps = steps or (8 if (hi - lo) % 8 == 0 else 6 if (hi - lo) % 6 == 0 else 4)
+    first = []
+    for src in sources:
+        chem_lo, mob_lo = chem_mob(src[lo - 2], src[lo - 1], src[lo], coef[lo - 1])
+        here, above = src[lo], src[lo + 1]
+        chem, mob = chem_mob(src[lo - 1], here, above, coef[lo])
+        first.append((here, above, chem, mob, (mob_lo + mob) * (chem - chem_lo)))
+
+    def step(i, states):
+        for j in range(steps):
+            k = lo + steps * i + j
+            coef_up = coef[k + 1]
+            after, values, forces = [], [], []
+            for src, (here, above, chem, mob, flux) in zip(sources, states):
+                top = src[k + 2]
+                chem_up, mob_up = chem_mob(here, above, top, coef_up)
+                flux_up = (mob + mob_up) * (chem_up - chem)
+                fy = (roll(mob, -1, 0) + mob) * (roll(chem, -1, 0) - chem)
+                fx = (roll(mob, -1, 1) + mob) * (roll(chem, -1, 1) - chem)
+                fx -= (roll(mob, 1, 1) + mob) * (chem - roll(chem, 1, 1))
+                total = (flux_up - flux) + (fy - roll(fy, 1, 0)) + fx
+                after.append((above, top, chem_up, mob_up, flux_up))
+                values.append(here)
+                forces.append(0.5 * total)
+            emit(k, *values, *forces)
+            states = tuple(after)
+        return states
+
+    lax.fori_loop(0, (hi - lo) // steps, step, tuple(first))
 
 
 def parities(shape):
@@ -92,14 +101,24 @@
     return out
 
 
-def coarse_flow(w, coef):
-    square = w * w
-    around = (roll(w, 2, 0) + roll(w, -2, 0)) + (roll(w, 2, 1) + roll(w, -2, 1))
-    chem = w * square - 0.25 * around
-    mob = coef * jnp.maximum(1.0 - square, 0.0)
+def coarse_sides(coef):
+    return coef, roll(coef, 2, 1), roll(coef, -2, 1)
+
+
+def coarse_chem_mob(left, here, right, coef):
+    square = here * here
+    around = (left + right) + (roll(here, 2, 0) + roll(here, -2, 0))
+    return here * square - 0.25 * around, coef * jnp.maximum(1.0 - square, 0.0)
+
+
+def coarse_flow(w, coefs):
+    left, right = roll(w, 2, 1), roll(w, -2, 1)
+    chem, mob = coarse_chem_mob(left, w, right, coefs[0])
+    chem_l, mob_l = coarse_chem_mob(roll(w, 4, 1), left, w, coefs[1])
+    chem_r, mob_r = coarse_chem_mob(w, right, roll(w, -4, 1), coefs[2])
+    fx = (mob_r + mob) * (chem_r - chem) - (mob + mob_l) * (chem - chem_l)
     fy = (roll(mob, -2, 0) + mob) * (roll(chem, -2, 0) - chem)
-    fx = (roll(mob, -2, 1) + mob) * (roll(chem, -2, 1) - chem)
-    return 0.125 * ((fy - roll(fy, 2, 0)) + (fx - roll(fx, 2, 1)))
+    return 0.125 * ((fy - roll(fy, 2, 0)) + fx)
 
 
 def kernel(
@@ -193,9 +212,9 @@
     for copy in mates:
         copy.wait_recv()
     top = own + 2 * planes
-    sweep(ui, ci, own + 2, top - 2, emit_mid)
-    sweep(mid, ci, own + 4, top - 4, emit_end)
-    sweep(end, ci, own + 6, top - 6, emit_quad)
+    sweep((ui,), ci, own + 2, top - 2, emit_mid)
+    sweep((mid,), ci, own + 4, top - 4, emit_end)
+    sweep((end,), ci, own + 6, top - 6, emit_quad)
 
     for arrived, passed in ((nears, mate_nears), (fars, mate_fars)):
         for i in range(2):
@@ -206,16 +225,16 @@
             copy.wait_recv()
         if arrived is nears:
             low = own - half
-            sweep(ui, ci, low + 2, own + 2, emit_mid)
-            sweep(ui, ci, top - 2, top + 2, emit_mid)
-            sweep(mid, ci, low + 4, own + 4, emit_end)
-            sweep(mid, ci, top - 4, top, emit_end)
-            sweep(end, ci, low + 6, own + 6, emit_quad)
-            sweep(end, ci, top - 6, top - 2, emit_quad)
+            sweep((ui,), ci, low + 2, own + 2, emit_mid)
+            sweep((ui,), ci, top - 2, top + 2, emit_mid)
+            sweep((mid,), ci, low + 4, own + 4, emit_end)
+            sweep((mid,), ci, top - 4, top, emit_end)
+            sweep((end,), ci, low + 6, own + 6, emit_quad)
+            sweep((end,), ci, top - 6, top - 2, emit_quad)
         else:
-            sweep(ui, ci, 2, low + 2, emit_mid)
-            sweep(mid, ci, 4, low + 4, emit_end)
-            sweep(end, ci, 6, low + 6, emit_quad)
+            sweep((ui,), ci, 2, low + 2, emit_mid)
+            sweep((mid,), ci, 4, low + 4, emit_end)
+            sweep((end,), ci, 6, low + 6, emit_quad)
 
     mine = list(range(own // 2, (own + planes) // 2))
     others = [q for q in range(3, (total - 6) // 2) if q not in mine]
@@ -226,7 +245,7 @@
             groups.append((group + group + group + group)[:4])
     own_groups = -(-len(mine) // 4)
 
-    coefs = [pack(ci, g, even_row, even_col) for g in groups]
+    coefs = [coarse_sides(pack(ci, g, even_row, even_col)) for g in groups]
     v0 = [pack(ui, g, even_row, even_col) for g in groups]
     v1 = [pack(end, g, even_row, even_col) for g in groups]
     force0 = [
@@ -254,31 +273,19 @@
                 node1[k] = mid[k] + by_mid[j]
                 node2[k] = end[k] + by_end[j]
 
-    def emit_f0(k, v, force):
-        quad[k] = force
-        mid2[k] = v + (DT * 5.0 / 24.0) * force
-        rest[k] = (-DT / 24.0) * force
-
-    sweep(start, ci, 8, total - 8, emit_f0)
-
-    def emit_f1(k, v, force):
-        mid2[k] = mid2[k] + (DT / 3.0) * force
-        rest[k] = rest[k] - (DT / 6.0) * force
-
-    sweep(node1, ci, 8, total - 8, emit_f1)
-
-    def emit_f2(k, v, force):
-        mid2[k] = mid2[k] - (DT / 24.0) * force
-        rest[k] = rest[k] + (DT * 5.0 / 24.0) * force
-
-    sweep(node2, ci, 8, total - 8, emit_f2)
+    def emit_mid2(k, v, _, __, f0, f1, f2):
+        quad[k] = f0
+        mid2[k] = v + ((DT * 5.0 / 24.0) * f0 + (DT / 3.0) * f1 - (DT / 24.0) * f2)
+        rest[k] = (DT * 5.0 / 24.0) * f2 - (DT / 24.0) * f0 - (DT / 6.0) * f1
+
+    sweep((start, node1, node2), ci, 8, total - 8, emit_mid2, 2)
 
     def emit_end2(k, v, force):
         quad[k] = quad[k] + 4.0 * force
         end[k] = v + (0.5 * DT) * force + rest[k]
 
-    sweep(mid2, ci, 10, total - 10, emit_end2)
-    sweep(end, ci, 12, total - 12, emit_quad)
+    sweep((mid2,), ci, 10, total - 10, emit_end2)
+    sweep((end,), ci, 12, total - 12, emit_quad)
 
     for i in range(own_groups):
         g = groups[i]

time: 28.4 us -> 25.3 us (0.89)
  Pallas kernels: 25.8 us -> 22.7 us
    pallas_call x1, Pallas kernels: 25.8 us -> 22.7 us  [on_device(): pl.pallas_call(functools.partial(kernel, n_tm, n_sp), out_shape=jax.Shape...]
where the time goes in v3:
time: 25.3 us; the launch traced here: 25.2 us
  Pallas kernels  22.7 us (90%)
  local copies, waits for them, and re-layouts  2.47 us (10%)
    pallas_call x1, Pallas kernels, on_device(): pl.pallas_call(functools.partial(kernel, n_tm, n_sp), out_shape=jax.Shape...  22.7 us
    unnamed x5, local copies, waits for them, and re-layouts  2.47 us

profile of v3, /device:TPU:17, one launch (start us, length us, event | category | flops | bytes accessed | tf_op | source)
XLA Modules:
  0.0 25.2 jit_solution(2118699974931672505)
XLA Ops:
  0.0 0.0 copy-start
  0.0 0.9 %copy-done = f32[8,8,512]{2,1,0:T(8,128)S(1)} copy-done((f32[8,8,512]{2,1,0:T(8,128)S(1)}, f32[8,8,512]{2,1,0:T(8,128)}, u32[]{:S(2)}) %copy-start) | copy-done | bytes 131096
  0.9 0.0 copy-start.1
  0.9 0.9 %copy-done.1 = f32[8,8,512]{2,1,0:T(8,128)S(1)} copy-done((f32[8,8,512]{2,1,0:T(8,128)S(1)}, f32[8,8,512]{2,1,0:T(8,128)}, u32[]{:S(2)}) %copy-start.1) | copy-done | bytes 131096
  1.8 22.7 %shard_map.28 = f32[8,8,512]{2,1,0:T(8,128)S(1)} custom-call(f32[8,8,512]{2,1,0:T(8,128)S(1)} %copy-done, f32[8,8,512]{2,1,0:T(8,128)S(1)} %copy-done.1), custom_call_target="tpu_custom_call" | custom-call | tf_op jit(solution)/shard_map/pallas_call | solution.py:351
  24.5 0.7 %copy.4 = f32[1,8,8,512]{3,2,1,0:T(8,128)} copy(f32[1,8,8,512]{3,2,1,0:T(8,128)S(1)} %bitcast.1) | data formatting | bytes 262144
Async XLA Ops:
  0.0 0.9 %copy-start = (f32[8,8,512]{2,1,0:T(8,128)S(1)}, f32[8,8,512]{2,1,0:T(8,128)}, u32[]{:S(2)}) copy-start(f32[8,8,512]{2,1,0:T(8,128)} %u_hbm.1) | copy-start | bytes 393220
  0.9 0.9 %copy-start.1 = (f32[8,8,512]{2,1,0:T(8,128)S(1)}, f32[8,8,512]{2,1,0:T(8,128)}, u32[]{:S(2)}) copy-start(f32[8,8,512]{2,1,0:T(8,128)} %c_hbm.1) | copy-start | bytes 393220

commit v4 on v3

--- a/solution.py
+++ b/solution.py
@@ -123,7 +123,7 @@
 
 def kernel(
     n_tm, n_sp, u_hbm, c_hbm, out, u, c, quad, mid, end, start, node1, node2, mid2, rest,
-    forcings, sp_send, sp_recv, own_sem, tm_send, tm_recv,
+    forcings, sp_send, sp_recv, own_sem, round_sem, tm_send, tm_recv,
 ):
     planes = u_hbm.shape[0]
     far = HALO - planes
@@ -141,13 +141,19 @@
     for peer in peers:
         pl.semaphore_signal(barrier, inc=1, device_id={"space": peer}, device_id_type=MESH)
 
-    def greet(d, carry):
-        pl.semaphore_signal(
-            barrier, inc=1, device_id={"tm": lax.rem(t + d, n_tm)}, device_id_type=MESH
-        )
-        return carry
-
-    lax.fori_loop(1, n_tm, greet, 0)
+    def greet(sem, d):
+        @pl.when(t >= d)
+        def _():
+            pl.semaphore_signal(sem, inc=1, device_id={"tm": t - d}, device_id_type=MESH)
+
+        @pl.when(t + d < n_tm)
+        def _():
+            pl.semaphore_signal(sem, inc=1, device_id={"tm": t + d}, device_id_type=MESH)
+
+    def greeted(d):
+        return (t >= d).astype(jnp.int32) + (t + d < n_tm).astype(jnp.int32)
+
+    greet(barrier, 1)
 
     local = [
         pltpu.make_async_copy(src, dst.at[pl.ds(own, planes)], own_sem.at[i])
@@ -155,7 +161,17 @@
     ]
     for copy in local:
         copy.start()
-    pl.semaphore_wait(barrier, len(peers) + n_tm - 1)
+    pl.semaphore_wait(barrier, len(peers) + greeted(1))
+    rounds = []
+    while 2**len(rounds) < n_tm - 1:
+        rounds.append(2**len(rounds))
+    greet(round_sem.at[0], 1)
+
+    def next_round(r):
+        if r < len(rounds):
+            pl.semaphore_wait(round_sem.at[r], greeted(rounds[r]))
+            if r + 1 < len(rounds):
+                greet(round_sem.at[r + 1], rounds[r + 1])
 
     def remote(f, kind, src, src_at, dst_at, rows, peer):
         return pltpu.make_async_remote_copy(
@@ -215,6 +231,7 @@
     sweep((ui,), ci, own + 2, top - 2, emit_mid)
     sweep((mid,), ci, own + 4, top - 4, emit_end)
     sweep((end,), ci, own + 6, top - 6, emit_quad)
+    next_round(0)
 
     for arrived, passed in ((nears, mate_nears), (fars, mate_fars)):
         for i in range(2):
@@ -231,6 +248,7 @@
             sweep((mid,), ci, top - 4, top, emit_end)
             sweep((end,), ci, low + 6, own + 6, emit_quad)
             sweep((end,), ci, top - 6, top - 2, emit_quad)
+            next_round(1)
         else:
             sweep((ui,), ci, 2, low + 2, emit_mid)
             sweep((mid,), ci, 4, low + 4, emit_end)
@@ -284,6 +302,8 @@
         quad[k] = quad[k] + 4.0 * force
         end[k] = v + (0.5 * DT) * force + rest[k]
 
+    for r in range(2, len(rounds)):
+        next_round(r)
     sweep((mid2,), ci, 10, total - 10, emit_end2)
     sweep((end,), ci, 12, total - 12, emit_quad)
 
@@ -359,6 +379,7 @@
                 pltpu.SemaphoreType.DMA((2, 5)),
                 pltpu.SemaphoreType.DMA((2, 5)),
                 pltpu.SemaphoreType.DMA((2,)),
+                pltpu.SemaphoreType.REGULAR((max(1, (n_tm - 1).bit_length()),)),
                 pltpu.SemaphoreType.DMA((n_tm,)),
                 pltpu.SemaphoreType.DMA((n_tm,)),
             ],

time: 25.3 us -> 24.1 us (0.953)
  Pallas kernels: 22.7 us -> 21.5 us
    pallas_call x1, Pallas kernels: 22.7 us -> 21.5 us  [on_device(): pl.pallas_call(functools.partial(kernel, n_tm, n_sp), out_shape=jax.Shape...]
where the time goes in v4:
time: 24.1 us; the launch traced here: 24 us
  Pallas kernels  21.5 us (89%)
  local copies, waits for them, and re-layouts  2.47 us (10%)
    pallas_call x1, Pallas kernels, on_device(): pl.pallas_call(functools.partial(kernel, n_tm, n_sp), out_shape=jax.Shape...  21.5 us
    unnamed x5, local copies, waits for them, and re-layouts  2.47 us

profile of v4, /device:TPU:17, one launch (start us, length us, event | category | flops | bytes accessed | tf_op | source)
XLA Modules:
  0.0 24.0 jit_solution(4186814443551800587)
XLA Ops:
  0.0 0.0 copy-start
  0.0 0.9 %copy-done = f32[8,8,512]{2,1,0:T(8,128)S(1)} copy-done((f32[8,8,512]{2,1,0:T(8,128)S(1)}, f32[8,8,512]{2,1,0:T(8,128)}, u32[]{:S(2)}) %copy-start) | copy-done | bytes 131096
  0.9 0.0 copy-start.1
  0.9 0.9 %copy-done.1 = f32[8,8,512]{2,1,0:T(8,128)S(1)} copy-done((f32[8,8,512]{2,1,0:T(8,128)S(1)}, f32[8,8,512]{2,1,0:T(8,128)}, u32[]{:S(2)}) %copy-start.1) | copy-done | bytes 131096
  1.8 21.5 %shard_map.28 = f32[8,8,512]{2,1,0:T(8,128)S(1)} custom-call(f32[8,8,512]{2,1,0:T(8,128)S(1)} %copy-done, f32[8,8,512]{2,1,0:T(8,128)S(1)} %copy-done.1), custom_call_target="tpu_custom_call" | custom-call | tf_op jit(solution)/shard_map/pallas_call | solution.py:371
  23.3 0.7 %copy.4 = f32[1,8,8,512]{3,2,1,0:T(8,128)} copy(f32[1,8,8,512]{3,2,1,0:T(8,128)S(1)} %bitcast.1) | data formatting | bytes 262144
Async XLA Ops:
  0.0 0.9 %copy-start = (f32[8,8,512]{2,1,0:T(8,128)S(1)}, f32[8,8,512]{2,1,0:T(8,128)}, u32[]{:S(2)}) copy-start(f32[8,8,512]{2,1,0:T(8,128)} %u_hbm.1) | copy-start | bytes 393220
  0.9 0.9 %copy-start.1 = (f32[8,8,512]{2,1,0:T(8,128)S(1)}, f32[8,8,512]{2,1,0:T(8,128)}, u32[]{:S(2)}) copy-start(f32[8,8,512]{2,1,0:T(8,128)} %c_hbm.1) | copy-start | bytes 393220
